TPU v7x, 32 devices: a whole 2x2x4 slice. The times are simulated.
32 devices in a mesh: groups: 2 (over y), layer: 4 (over z), token: 2 (over x), width: 2 (over core).
Axes of the slice: x: 2, y: 2, z: 4, core: 2. Of those that a mesh axis runs over, the one named last changes fastest.
Arguments:
- source_acts: bfloat16 [8, 1024, 4096], P('layer', 'groups', ('token', 'width')), parts along dimension 1, may hold values from -6 to 6
- enc_weight: bfloat16 [8, 4096, 128], P('layer', ('token', 'width')), may hold values from -0.09375 to 0.09375
- enc_offset: float32 [8, 128], P('layer'), may hold values from -4 to 4
- topk_latents: int32 [8, 1024, 64], P('layer', 'groups'), parts along dimension 1, may hold values from 0 to 127, all different within a row
- pair_table: int32 [36, 2], P('layer'), may hold values from 0 to 7, as said below
- dec_weight: bfloat16 [36, 128, 4096], P('layer', None, ('token', 'width')), may hold values from -0.25 to 0.25
- target_acts: bfloat16 [8, 1024, 4096], P('layer', 'groups', ('token', 'width')), parts along dimension 1, may hold values from -6 to 6
Outputs:
- dec_gradient: bfloat16 [72, 128, 4096], P(('groups', 'layer'), None, ('token', 'width')), parts along dimension 0
- enc_gradient: float32 [16, 4096, 128], P(('groups', 'layer'), ('token', 'width')), parts along dimension 0
There are 2 independent parts, one for each index of `groups`. A program takes and returns all parts, laid end to end along the dimension named above; an argument that names none is the same for every part. Nothing has to cross between parts.
Inputs may be any that keep to these rules, and one draw needn't show every extreme that they name: `topk_latents`: each row names 64 different latents. `pair_table`: each pair (s, m) with s <= m appears once; every group of 9 consecutive rows holds all pairs whose target is f or 7 - f, for one f below 4, in any order.
All inputs are finite; a program needn't handle non-finite values.
Results may differ from a plain program's by a relative error of at most 0.0049.
Values may be sent and summed in bfloat16 or wider, within the bound.
A program may use at most 128 MiB of HBM per device.

v0:
```python
import jax
import jax.numpy as jnp
from jax import lax
from jax.sharding import PartitionSpec as P

grad_scale = 1.0 / 32.0


def active_mask(chosen, latent_total):
    columns = lax.broadcasted_iota(jnp.int32, (1, 1, 1, latent_total), 3)
    return jnp.sum((chosen[..., None] == columns).astype(jnp.float32), axis=2)


def shards(source_acts, enc_weight, enc_offset, topk_latents, pair_table, dec_weight, target_acts):
    latent_width = enc_weight.shape[2]
    partial_value = jnp.einsum(
        "ltd,ldk->ltk", source_acts, enc_weight, preferred_element_type=jnp.float32
    )
    preact = lax.psum(partial_value, ("token", "width")) + enc_offset[:, None, :]
    picked = active_mask(topk_latents, latent_width)
    latents = (picked * jax.nn.softplus(preact)).astype(jnp.bfloat16)
    every_latent = lax.all_gather(latents, "layer", axis=0, tiled=True)
    layer_total = every_latent.shape[0]
    source_ids = pair_table[:, 0]
    target_ids = pair_table[:, 1]
    upper_slot = target_ids == jnp.max(target_ids)
    slot_mask = upper_slot.astype(jnp.float32)
    paired = every_latent[source_ids]
    contrib = jnp.einsum("ptk,pkd->ptd", paired, dec_weight, preferred_element_type=jnp.float32)
    higher = jnp.sum(contrib * slot_mask[:, None, None], axis=0)
    lower_sum = jnp.sum(contrib * (1.0 - slot_mask)[:, None, None], axis=0)
    rebuilt = jnp.stack([lower_sum, higher])
    error_grad = ((rebuilt - target_acts.astype(jnp.float32)) * grad_scale).astype(jnp.bfloat16)
    err_pair = jnp.where(upper_slot[:, None, None], error_grad[1][None], error_grad[0][None])
    dec_gradient = jnp.einsum(
        "ptk,ptd->pkd", paired, err_pair, preferred_element_type=jnp.float32
    ).astype(jnp.bfloat16)
    back_pair = jnp.einsum("ptd,pkd->ptk", err_pair, dec_weight, preferred_element_type=jnp.float32)
    layer_ids = lax.broadcasted_iota(jnp.int32, (1, layer_total), 1)
    onehot = (source_ids[:, None] == layer_ids).astype(jnp.float32)
    spread = jnp.einsum("pl,ptk->ltk", onehot, back_pair, precision=lax.Precision.HIGHEST)
    own_rows = lax.psum_scatter(spread, "layer", scatter_dimension=0, tiled=True)
    latent_grad = lax.psum(own_rows, ("token", "width"))
    pre_grad = (latent_grad * picked * jax.nn.sigmoid(preact)).astype(jnp.bfloat16)
    enc_gradient = jnp.einsum(
        "ltd,ltk->ldk", source_acts, pre_grad, preferred_element_type=jnp.float32
    )
    return (dec_gradient, enc_gradient)


def solution(mesh):
    in_specs = (
        P("layer", "groups", ("token", "width")),
        P("layer", ("token", "width"), None),
        P("layer", None),
        P("layer", "groups", None),
        P("layer", None),
        P("layer", None, ("token", "width")),
        P("layer", "groups", ("token", "width")),
    )
    out_specs = (
        P(("groups", "layer"), None, ("token", "width")),
        P(("groups", "layer"), ("token", "width"), None),
    )
    return jax.shard_map(shards, mesh=mesh, in_specs=in_specs, out_specs=out_specs, check_vma=False)
```

profile of v0, /device:TPU:1, one launch (start us, length us, event | category | flops | bytes accessed | tf_op | source)
XLA Modules:
  0.0 182.8 jit_solution(8098299509691810652)
XLA Ops:
  7.2 0.0 all-reduce.3.cloned.1.call-start
  7.2 3.3 %fusion.27 = f32[2,512,128]{2,1,0:T(8,128)} fusion(bf16[2,512,1024]{2,1,0:T(8,128)(2,1)} %param.7, bf16[2,1024,128]{2,1,0:T(8,128)(2,1)} %param.8), kind=kOutput, calls=%fused_computation.42 | convolution fusion | flops 268435456 | bytes 3145728 | tf_op jit(solution)/shard_map/ltd,ldk->ltk/dot_general | solution.py:16
  10.6 0.0 all-gather.2.cloned.1.call-start
  10.7 0.2 copy.17
  10.9 11.3 %convert_reduce_fusion = f32[2,512,128]{2,1,0:T(8,128)S(1)} fusion(s32[2,512,64]{2,1,0:T(8,128)S(1)} %copy.17), kind=kLoop, calls=%fused_computation.1 | loop fusion | flops 25034752 | bytes 786432 | tf_op jit(solution)/shard_map/reduce_sum | solution.py:11
  22.2 22.6 %all-reduce.3.cloned.1.call-done = f32[2,512,128]{2,1,0:T(8,128)} async-done(((f32[2,512,128]{2,1,0:T(8,128)}), f32[2,512,128]{2,1,0:T(8,128)}) %all-reduce.3.cloned.1.call-update) | async-done | bytes 524304 | tf_op jit(solution)/shard_map/psum | solution.py:19
  44.8 2.1 %fusion.18 = bf16[2,512,128]{2,1,0:T(8,128)(2,1)} fusion(f32[2,512,128]{2,1,0:T(8,128)S(1)} %convert_reduce_fusion, f32[2,512,128]{2,1,0:T(8,128)} %all-reduce.3.cloned.1.call-done, f32[2,128]{1,0:T(2,128)S(1)} %copy-done.6), kind=kLoop, calls=%fused_computation.26 | loop fusion | flops 1179648 | bytes 1311744 | tf_op jit(solution)/shard_map/convert_element_type | solution.py:21
  46.9 0.0 reduce-scatter.2.cloned.1.call-start
  46.9 0.6 slice_bitcast_fusion.2
  47.6 0.7 fusion.26
  48.3 28.1 %all-gather.2.cloned.1.call-done = bf16[8,512,128]{2,1,0:T(8,128)(2,1)} async-done(((bf16[2,512,128]{2,1,0:T(8,128)(2,1)}), bf16[8,512,128]{2,1,0:T(8,128)(2,1)}) %all-gather.2.cloned.1.call-update) | async-done | bytes 1048592 | tf_op jit(solution)/shard_map/all_gather | solution.py:22
  76.3 3.0 %gather_fusion = bf16[9,512,128]{2,1,0:T(8,128)(2,1)} fusion(bf16[8,512,128]{2,1,0:T(8,128)(2,1)} %all-gather.2.cloned.1.call-done, s32[1024]{0:T(1024)S(1)} %pad_clamp_fusion), kind=kCustom, calls=%fused_computation | custom fusion | bytes 2359332 | tf_op jit(solution)/shard_map/gather | solution.py:28
  79.4 5.7 %multiply_reduce_fusion.1 = (f32[512,1024]{1,0:T(8,128)S(1)}, f32[512,1024]{1,0:T(8,128)S(1)}) fusion(f32[9]{0:T(128)S(1)} %broadcast_subtract_fusion, f32[9]{0:T(128)S(1)} %get-tuple-element.10, bf16[9,512,128]{2,1,0:T(8,128)(2,1)} %gather_fusion, bf16[9,128,1024]{2,1,0:T(8,128)(2,1)S(1)} %copy-done), kind=kOutput, calls=%fused_computation.4 | convolution fusion | flops 1225785344 | bytes 7733320 | tf_op jit(solution)/shard_map/ptk,pkd->ptd/dot_general | solution.py:29
  85.1 0.8 fusion.11
  85.9 0.2 slice_bitcast_fusion.1
  86.1 2.8 %fusion = f32[9,512,128]{2,1,0:T(8,128)S(1)} fusion(bf16[9,128,1024]{2,1,0:T(8,128)(2,1)S(1)} %copy-done, pred[9]{0:T(512)(128)(4,1)S(1)} %get-tuple-element.11, bf16[512,1024]{1,0:T(8,128)(2,1)S(1)} %get-tuple-element.13, bf16[512,1024]{1,0:T(8,128)(2,1)S(1)} %get-tuple-element.12), kind=kOutput, calls=%fused_computation.5 | convolution fusion | flops 1212678144 | bytes 6815753 | tf_op jit(solution)/shard_map/ptd,pkd->ptk/dot_general | solution.py:38
  88.9 2.8 %fusion.12 = f32[8,512,128]{2,0,1:T(8,128)S(1)} fusion(f32[9,512,128]{2,1,0:T(8,128)S(1)} %fusion, s32[9]{0:T(128)S(1)} %get-tuple-element.14), kind=kOutput, calls=%fused_computation.18 | convolution fusion | flops 56623176 | bytes 4456484 | tf_op jit(solution)/shard_map/pl,ptk->ltk/dot_general | solution.py:41
  91.7 1.7 copy.20
  93.4 0.0 all-reduce.5.cloned.1.call-start
  93.5 43.5 %reduce-scatter.2.cloned.1.call-done = f32[2,512,128]{2,1,0:T(8,128)} async-done(((f32[8,512,128]{2,1,0:T(8,128)}), f32[2,512,128]{2,1,0:T(8,128)}) %reduce-scatter.2.cloned.1.call-update) | async-done | bytes 524304 | tf_op jit(solution)/shard_map/reduce_scatter | solution.py:42
  137.0 5.0 %fusion.14 = bf16[9,128,1024]{2,1,0:T(8,128)(2,1)} fusion(bf16[9,512,128]{2,1,0:T(8,128)(2,1)} %gather_fusion, pred[9]{0:T(512)(128)(4,1)S(1)} %get-tuple-element.11, bf16[512,1024]{1,0:T(8,128)(2,1)} %copy-done.4, bf16[512,1024]{1,0:T(8,128)(2,1)} %copy-done.3), kind=kOutput, calls=%fused_computation.20 | convolution fusion | flops 1213857792 | bytes 5636105 | tf_op jit(solution)/shard_map/ptk,ptd->pkd/dot_general | solution.py:35
  141.9 28.5 %all-reduce.5.cloned.1.call-done = f32[2,512,128]{2,1,0:T(8,128)} async-done(((f32[2,512,128]{2,1,0:T(8,128)}), f32[2,512,128]{2,1,0:T(8,128)}) %all-reduce.5.cloned.1.call-update) | async-done | bytes 524304 | tf_op jit(solution)/shard_map/psum | solution.py:43
  170.4 3.3 %convolution_bitcast_fusion = f32[2,1024,128]{1,2,0:T(8,128)} fusion(bf16[2,512,1024]{2,1,0:T(8,128)(2,1)} %param.7, f32[2,512,128]{2,1,0:T(8,128)} %all-reduce.5.cloned.1.call-done, f32[2,512,128]{2,1,0:T(8,128)S(1)} %convert_reduce_fusion, f32[2,512,128]{2,1,0:T(8,128)S(1)} %copy-done.1, f32[2,128]{1,0:T(2,128)S(1)} %copy-done.6), kind=kOutput, calls=%fused_computation.22 | convolution fusion | flops 269352960 | bytes 4719616 | tf_op jit(solution)/shard_map/ltd,ltk->ldk/dot_general | solution.py:45
  173.7 2.5 %copy.22 = f32[2,1024,128]{2,1,0:T(8,128)} copy(f32[2,1024,128]{1,2,0:T(8,128)} %convolution_bitcast_fusion) | data formatting | bytes 2097152
  (22 shorter events, 0.1 us)
Async XLA Ops:
  7.2 72.2 %copy-start = (bf16[9,128,1024]{2,1,0:T(8,128)(2,1)S(1)}, bf16[9,128,1024]{2,1,0:T(8,128)(2,1)}, u32[]{:S(2)}) copy-start(bf16[9,128,1024]{2,1,0:T(8,128)(2,1)} %param.12) | copy-start | bytes 7077892
  7.2 3.5 %copy-start.5 = (s32[2,512,64]{1,2,0:T(8,128)S(1)}, s32[2,512,64]{1,2,0:T(8,128)}, u32[]{:S(2)}) copy-start(s32[2,512,64]{1,2,0:T(8,128)} %param.10) | copy-start | bytes 786436
  7.2 37.6 %copy-start.6 = (f32[2,128]{1,0:T(2,128)S(1)}, f32[2,128]{1,0:T(2,128)}, u32[]{:S(2)}) copy-start(f32[2,128]{1,0:T(2,128)} %param.9) | copy-start | bytes 3076
  7.2 37.6 %all-reduce.3.cloned.1.call-start = ((), (), s32[]{:S(2)}) async-start(), calls=%async_computation.1 | async-start | bytes 1048576 | tf_op jit(solution)/shard_map/psum | solution.py:19
  10.6 36.4 %copy-start.7 = (s32[9,2]{0,1:T(2,128)S(1)}, s32[9,2]{0,1:T(2,128)}, u32[]{:S(2)}) copy-start(s32[9,2]{0,1:T(2,128)} %param.11) | copy-start | bytes 220
  10.6 65.7 %all-gather.2.cloned.1.call-start = ((), (), s32[]{:S(2)}) async-start(), calls=%async_computation.2 | async-start | bytes 1310720 | tf_op jit(solution)/shard_map/all_gather | solution.py:22
  46.9 90.0 %reduce-scatter.2.cloned.1.call-start = ((), (), s32[]{:S(2)}) async-start(), calls=%async_computation.3 | async-start | bytes 2621440 | tf_op jit(solution)/shard_map/reduce_scatter | solution.py:42
  79.4 5.7 %copy-start.2 = (bf16[2,512,1024]{2,1,0:T(8,128)(2,1)S(1)}, bf16[2,512,1024]{2,1,0:T(8,128)(2,1)}, u32[]{:S(2)}) copy-start(bf16[2,512,1024]{2,1,0:T(8,128)(2,1)} %param.13) | copy-start | bytes 6291460
  86.1 2.8 %copy-start.3 = (bf16[512,1024]{1,0:T(8,128)(2,1)}, bf16[512,1024]{1,0:T(8,128)(2,1)S(1)}, u32[]{:S(2)}) copy-start(bf16[512,1024]{1,0:T(8,128)(2,1)S(1)} %get-tuple-element.12) | copy-start | bytes 3145732
  86.1 2.8 %copy-start.4 = (bf16[512,1024]{1,0:T(8,128)(2,1)}, bf16[512,1024]{1,0:T(8,128)(2,1)S(1)}, u32[]{:S(2)}) copy-start(bf16[512,1024]{1,0:T(8,128)(2,1)S(1)} %get-tuple-element.13) | copy-start | bytes 3145732
  93.4 77.0 %all-reduce.5.cloned.1.call-start = ((), (), s32[]{:S(2)}) async-start(), calls=%async_computation.4 | async-start | bytes 1048576 | tf_op jit(solution)/shard_map/psum | solution.py:43
  136.9 33.5 %copy-start.1 = (f32[2,512,128]{2,1,0:T(8,128)S(1)}, f32[2,512,128]{2,1,0:T(8,128)}, u32[]{:S(2)}) copy-start(f32[2,512,128]{2,1,0:T(8,128)} %all-reduce.3.cloned.1.call-done) | copy-start | bytes 1572868
Sparse Core Ops, SparseCore 0:
  11.0 33.7 all-reduce.2
  47.0 29.2 all-gather.1
  93.5 43.3 reduce-scatter.1
  139.2 31.1 all-reduce.4
where the time goes:
time: 185 us; the launch traced here: 183 us
  waiting for transfers between devices  123 us (66%)
  matrix products  22.8 us (12%)
  other arithmetic  15.5 us (8%)
  between operations  13.9 us (8%)
  local copies, waits for them, and re-layouts  7.66 us (4%)
    reduce_scatter x1, waiting for transfers between devices, shards(): lax.psum_scatter(spread, 'layer', scatter_dimension=0, tiled=True)  43.5 us
    psum x1, waiting for transfers between devices, shards(): latent_grad = lax.psum(own_rows, ('token', 'width'))  28.5 us
    all_gather x1, waiting for transfers between devices, shards(): every_latent = lax.all_gather(latents, 'layer', axis=0, tiled=True)  28.1 us
    psum x1, waiting for transfers between devices, shards(): lax.psum(partial_value, ('token', 'width')) + enc_offset[:, None, :]  22.6 us
    reduce_sum x1, other arithmetic, active_mask(): return jnp.sum((chosen[..., None] == columns).astype(jnp.float32), axis=2)  11.3 us
    dot_general x1, matrix products, shards(): jnp.einsum('ptk,pkd->ptd', paired, dec_weight, preferred_element_type=jnp...  5.72 us
    dot_general x1, matrix products, shards(): jnp.einsum('ptk,ptd->pkd', paired, err_pair, preferred_element_type=jnp.f...  4.96 us
  transfers between devices with their start and end apart: 4, of which 4 were waited for; matrix products, arithmetic and copies ran while one was open for 10% of the time, Pallas kernels for 0%

commit v1 on v0

v1 whole, which is shorter than its diff:
```python
import functools

import jax
import jax.numpy as jnp
from jax import lax
from jax.experimental import pallas as pl
from jax.experimental.pallas import tpu as pltpu
from jax.sharding import PartitionSpec as P

grad_scale = 1.0 / 32.0
MESH = pl.DeviceIdType.MESH
F32 = jnp.float32
BF16 = jnp.bfloat16


def kernel(
    dims,
    source_hbm, encw_hbm, offset_hbm, topk_hbm, table, decw_hbm, target_hbm,
    decgrad_hbm, encgrad_hbm,
    source, source_t, encw, offset, topk, decw, target,
    part, part_core, part_x, preact, picked, lat, err,
    back, back_core, back_xs, back_x, back_zs, back_z, pre_grad, dec_out, enc_out,
    high_pair, low_pair, slot_of,
    in_sem, out_sem,
    pc_s, pc_r, px_s, px_r, lz_s, lz_r, lx_s, lx_r, lc_s, lc_r,
    bc_s, bc_r, bx_s, bx_r, bz_s, bz_r, gx_s, gx_r, gc_s, gc_r,
):
    layers, n_z, n_t, own, tokens, width, latents, pairs = dims
    half = tokens // 2
    chunk = half // n_t
    z = lax.axis_index("layer")
    t = lax.axis_index("token")
    w = lax.axis_index("width")
    other = 1 - w

    def half_rows(core):
        return pl.ds(pl.multiple_of(core * half, half), half)

    def chunk_rows(tok, core):
        return pl.ds(pl.multiple_of(core * half + tok * chunk, chunk), chunk)

    def x_peer(d):
        return lax.rem(t + d, n_t)

    def z_peer(d):
        return lax.rem(z + d, n_z)

    def z_from(d):
        return lax.rem(z - d + n_z, n_z)

    def z_layers(zz):
        return pl.ds(zz * own, own)

    my_half = half_rows(w)
    my_rows = chunk_rows(t, w)
    sends = []

    def remote(src, dst, ssem, rsem, **where):
        copy = pltpu.make_async_remote_copy(
            src_ref=src, dst_ref=dst, send_sem=ssem, recv_sem=rsem,
            device_id=where, device_id_type=MESH,
        )
        copy.start()
        sends.append(copy)
        return copy

    loads = {}

    def load(name, src, dst, sem):
        loads[name] = pltpu.make_async_copy(src, dst, in_sem.at[sem])
        loads[name].start()

    for l in range(own):
        load(("s", l), source_hbm.at[l], source.at[l], 2 * l)
        load(("e", l), encw_hbm.at[l], encw.at[l], 2 * l + 1)
    load("topk", topk_hbm.at[:, my_rows], topk, 2 * own)
    load("offset", offset_hbm, offset, 2 * own + 1)
    load("decw", decw_hbm, decw.at[pl.ds(0, pairs)], 2 * own + 2)
    load("target", target_hbm, target, 2 * own + 3)

    barrier = pltpu.get_barrier_semaphore()
    pl.semaphore_signal(barrier, inc=1, device_id={"width": other}, device_id_type=MESH)
    for d in range(1, n_t):
        pl.semaphore_signal(barrier, inc=1, device_id={"token": x_peer(d)}, device_id_type=MESH)
    for d in range(1, n_z):
        pl.semaphore_signal(barrier, inc=1, device_id={"layer": z_peer(d)}, device_id_type=MESH)

    core_copies = []
    for l in range(own):
        loads[("s", l)].wait()
        loads[("e", l)].wait()
        part[l] = jnp.dot(source[l], encw[l], preferred_element_type=F32)
        if l == 0:
            pl.semaphore_wait(barrier, n_t + n_z - 1)
        core_copies.append(remote(
            part.at[l, half_rows(other)], part_core.at[l], pc_s.at[l], pc_r.at[l], width=other))
    x_copies = []
    for l in range(own):
        core_copies[l].wait_recv()
        part[l, my_half, :] = part[l, my_half, :] + part_core[l]
        for d in range(1, n_t):
            x_copies.append(remote(
                part.at[l, chunk_rows(x_peer(d), w)], part_x.at[l, d - 1],
                px_s.at[l, d - 1], px_r.at[l, d - 1], token=x_peer(d)))

    loads["topk"].wait()
    loads["offset"].wait()
    block = 32

    for l in range(own):
        @pl.loop(0, chunk // block)
        def _(i, l=l):
            rows = pl.ds(pl.multiple_of(i * block, block), block)
            ids = topk[l, rows, :]
            columns = lax.broadcasted_iota(jnp.int32, (block, latents), 1)
            hit = jnp.zeros((block, latents), F32)
            for k in range(topk.shape[2]):
                hit = jnp.where(ids[:, k : k + 1] == columns, 1.0, hit)
            picked[l, rows, :] = hit

    high_target = table[0, 1]
    for p in range(1, pairs):
        high_target = jnp.maximum(high_target, table[p, 1])
    for p in range(pairs):
        slot_of[p] = (table[p, 1] == high_target).astype(jnp.int32)

    @pl.loop(0, layers)
    def _(l):
        high = jnp.int32(pairs)
        low = jnp.int32(pairs)
        for p in range(pairs):
            same = table[p, 0] == l
            up = table[p, 1] == high_target
            high = jnp.where(jnp.logical_and(same, up), p, high)
            low = jnp.where(jnp.logical_and(same, jnp.logical_not(up)), p, low)
        high_pair[l] = high
        low_pair[l] = low

    for l in range(own):
        pre = part[l, my_rows, :] + offset[pl.ds(l, 1), :]
        for d in range(1, n_t):
            x_copies[l * (n_t - 1) + d - 1].wait_recv()
            pre = pre + part_x[l, d - 1]
        preact[l] = pre
        soft = jnp.maximum(pre, 0.0) + jnp.log1p(jnp.exp(-jnp.abs(pre)))
        lat[z * own + l, my_rows, :] = (picked[l] * soft).astype(BF16)

    z_copies = [None]
    for d in range(1, n_z):
        here = lat.at[z_layers(z), my_rows]
        z_copies.append(remote(here, here, lz_s.at[d - 1], lz_r.at[d - 1], layer=z_peer(d)))
    x_copies = []
    for j in range(n_z):
        if j:
            z_copies[j].wait_recv()
        for d in range(1, n_t):
            here = lat.at[z_layers(z_from(j)), my_rows]
            x_copies.append(remote(
                here, here, lx_s.at[j, d - 1], lx_r.at[j, d - 1], token=x_peer(d)))
    loads["decw"].wait()
    decw[pairs] = jnp.zeros((latents, width), BF16)
    core_copies = []
    for j in range(n_z):
        for d in range(1, n_t):
            x_copies[j * (n_t - 1) + d - 1].wait_recv()
        here = lat.at[z_layers(z_from(j)), my_half]
        core_copies.append(remote(here, here, lc_s.at[j], lc_r.at[j], width=other))
    for l in range(own):
        source_t[l] = source[l].T
    loads["target"].wait()
    for j in range(n_z):
        core_copies[j].wait_recv()

    tile = 256
    lows = layers // 2

    @pl.loop(0, width // tile)
    def _(n):
        cols = pl.ds(pl.multiple_of(n * tile, tile), tile)
        for slot, count, pair_of in ((1, layers, high_pair), (0, lows, low_pair)):
            acts = jnp.concatenate([lat[l] for l in range(count)], axis=1)
            weight = jnp.concatenate([decw[pair_of[l], :, cols] for l in range(count)], axis=0)
            rebuilt = jnp.dot(acts, weight, preferred_element_type=F32)
            goal = target[slot, :, cols].astype(F32)
            err[slot, :, cols] = ((rebuilt - goal) * grad_scale).astype(BF16)

    order = list(range(1, n_z)) + [0]
    core_copies = {}
    for j in order:
        zz = z_peer(j)
        weight = jnp.concatenate(
            [
                jnp.concatenate([decw[high_pair[zz * own + i]], decw[low_pair[zz * own + i]]], axis=1)
                for i in range(own)
            ],
            axis=0,
        )
        both = jnp.concatenate([err[1], err[0]], axis=1)
        spread = lax.dot_general(
            both, weight, (((1,), (1,)), ((), ())), preferred_element_type=F32)
        for i in range(own):
            back[j, i] = spread[:, i * latents : (i + 1) * latents]
        core_copies[j] = remote(
            back.at[j, :, half_rows(other)], back_core.at[j], bc_s.at[j], bc_r.at[j], width=other)
    x_copies = {}
    for j in order:
        core_copies[j].wait_recv()
        total = back[j, :, my_half, :] + back_core[j]
        back[j, :, my_half, :] = total
        back_xs[j] = total.astype(BF16)
        for d in range(1, n_t):
            rows = pl.ds(pl.multiple_of(x_peer(d) * chunk, chunk), chunk)
            x_copies[j, d] = remote(
                back_xs.at[j, :, rows], back_x.at[j, d - 1],
                bx_s.at[j, d - 1], bx_r.at[j, d - 1], token=x_peer(d))

    def dec_gradient(first, last):
        @pl.loop(first, last)
        def _(p):
            acts = lat[table[p, 0]].T
            grad = jnp.dot(acts, err[slot_of[p]], preferred_element_type=F32)
            dec_out[p] = grad.astype(BF16)
            pltpu.make_async_copy(dec_out.at[p], decgrad_hbm.at[p], out_sem.at[p]).start()

    middle = pairs // 2
    dec_gradient(0, middle)
    z_copies = {}
    for j in order:
        total = back[j, :, my_rows, :]
        for d in range(1, n_t):
            x_copies[j, d].wait_recv()
            total = total + back_x[j, d - 1].astype(F32)
        if j:
            back_zs[j - 1] = total.astype(BF16)
            z_copies[j] = remote(
                back_zs.at[j - 1], back_z.at[j - 1], bz_s.at[j - 1], bz_r.at[j - 1], layer=z_peer(j))
        else:
            mine = total
    dec_gradient(middle, pairs)
    for j in range(1, n_z):
        z_copies[j].wait_recv()
        mine = mine + back_z[j - 1].astype(F32)
    for l in range(own):
        pre_grad[l, my_rows, :] = (mine[l] * picked[l] * jax.nn.sigmoid(preact[l])).astype(BF16)

    here = pre_grad.at[:, my_rows]
    x_copies = [
        remote(here, here, gx_s.at[d - 1], gx_r.at[d - 1], token=x_peer(d)) for d in range(1, n_t)
    ]
    for copy in x_copies:
        copy.wait_recv()
    here = pre_grad.at[:, my_half]
    remote(here, here, gc_s.at[0], gc_r.at[0], width=other).wait_recv()
    for l in range(own):
        enc_out[l] = jnp.dot(source_t[l], pre_grad[l], preferred_element_type=F32)
        pltpu.make_async_copy(enc_out.at[l], encgrad_hbm.at[l], out_sem.at[pairs + l]).start()
    for copy in sends:
        copy.wait_send()

    @pl.loop(0, pairs)
    def _(p):
        pltpu.make_async_copy(dec_out.at[p], decgrad_hbm.at[p], out_sem.at[p]).wait()

    for l in range(own):
        pltpu.make_async_copy(enc_out.at[l], encgrad_hbm.at[l], out_sem.at[pairs + l]).wait()


def shards(n_z, n_t, source_acts, enc_weight, enc_offset, topk_latents, pair_table, dec_weight, target_acts):
    own, tokens, width = source_acts.shape
    latents = enc_weight.shape[2]
    pairs = pair_table.shape[0]
    topk = topk_latents.shape[2]
    layers = own * n_z
    half = tokens // 2
    chunk = half // n_t
    peers = max(n_t - 1, 1)
    others = max(n_z - 1, 1)
    dims = (layers, n_z, n_t, own, tokens, width, latents, pairs)
    dma = pltpu.SemaphoreType.DMA
    scratch = [
        pltpu.VMEM((own, tokens, width), BF16),
        pltpu.VMEM((own, width, tokens), BF16),
        pltpu.VMEM((own, width, latents), BF16),
        pltpu.VMEM((own, latents), F32),
        pltpu.VMEM((own, chunk, topk), jnp.int32),
        pltpu.VMEM((pairs + 1, latents, width), BF16),
        pltpu.VMEM((2, tokens, width), BF16),
        pltpu.VMEM((own, tokens, latents), F32),
        pltpu.VMEM((own, half, latents), F32),
        pltpu.VMEM((own, peers, chunk, latents), F32),
        pltpu.VMEM((own, chunk, latents), F32),
        pltpu.VMEM((own, chunk, latents), F32),
        pltpu.VMEM((layers, tokens, latents), BF16),
        pltpu.VMEM((2, tokens, width), BF16),
        pltpu.VMEM((n_z, own, tokens, latents), F32),
        pltpu.VMEM((n_z, own, half, latents), F32),
        pltpu.VMEM((n_z, own, half, latents), BF16),
        pltpu.VMEM((n_z, peers, own, chunk, latents), BF16),
        pltpu.VMEM((others, own, chunk, latents), BF16),
        pltpu.VMEM((others, own, chunk, latents), BF16),
        pltpu.VMEM((own, tokens, latents), BF16),
        pltpu.VMEM((pairs, latents, width), BF16),
        pltpu.VMEM((own, width, latents), F32),
        pltpu.SMEM((layers,), jnp.int32),
        pltpu.SMEM((layers,), jnp.int32),
        pltpu.SMEM((pairs,), jnp.int32),
        dma((2 * own + 4,)),
        dma((pairs + own,)),
    ]
    for shape in (
        (own,), (own, peers), (others,), (n_z, peers), (n_z,),
        (n_z,), (n_z, peers), (others,), (peers,), (1,),
    ):
        scratch += [dma(shape), dma(shape)]
    hbm = pl.BlockSpec(memory_space=pl.ANY)
    return pl.pallas_call(
        functools.partial(kernel, dims),
        out_shape=(
            jax.ShapeDtypeStruct((pairs, latents, width), BF16),
            jax.ShapeDtypeStruct((own, width, latents), F32),
        ),
        in_specs=[hbm, hbm, hbm, hbm, pl.BlockSpec(memory_space=pltpu.SMEM), hbm, hbm],
        out_specs=(hbm, hbm),
        scratch_shapes=scratch,
        compiler_params=pltpu.CompilerParams(
            collective_id=0, has_side_effects=True, vmem_limit_bytes=56 * 1024 * 1024
        ),
        cost_estimate=pl.CostEstimate(
            flops=2 * tokens * width * latents * (4 * pairs + 2 * own),
            bytes_accessed=2 * (2 * pairs * latents * width + 4 * tokens * width * own),
            transcendentals=0,
        ),
        name="transcoder_step",
    )(source_acts, enc_weight, enc_offset, topk_latents, pair_table, dec_weight, target_acts)


def solution(mesh):
    in_specs = (
        P("layer", "groups", ("token", "width")),
        P("layer", ("token", "width"), None),
        P("layer", None),
        P("layer", "groups", None),
        P("layer", None),
        P("layer", None, ("token", "width")),
        P("layer", "groups", ("token", "width")),
    )
    out_specs = (
        P(("groups", "layer"), None, ("token", "width")),
        P(("groups", "layer"), ("token", "width"), None),
    )
    body = functools.partial(shards, mesh.shape["layer"], mesh.shape["token"])
    return jax.shard_map(body, mesh=mesh, in_specs=in_specs, out_specs=out_specs, check_vma=False)
```

time: 185 us -> 57.5 us (0.31); the launches traced: 183 us -> 57.3 us
  waiting for transfers between devices: 123 us -> 0 us
  Pallas kernels: 0 us -> 49 us
  matrix products: 22.8 us -> 0 us
  other arithmetic: 15.5 us -> 0 us
  between operations: 13.9 us -> 0.65 us
    psum x2 -> x0, waiting for transfers between devices: 51.1 us -> none  [the longest x1 28.5 us: shards(): latent_grad = lax.psum(own_rows, ('token', 'width'))]
    pallas_call x0 -> x1, Pallas kernels: none -> 49 us  [shards(): pl.pallas_call(functools.partial(kernel, dims), out_shape=(jax.ShapeDtype...]
    reduce_scatter x1 -> x0, waiting for transfers between devices: 43.5 us -> none  [shards(): lax.psum_scatter(spread, 'layer', scatter_dimension=0, tiled=True)]
    all_gather x1 -> x0, waiting for transfers between devices: 28.1 us -> none  [shards(): every_latent = lax.all_gather(latents, 'layer', axis=0, tiled=True)]
    dot_general x6 -> x0, matrix products: 22.8 us -> none  [the longest x1 5.72 us: shards(): jnp.einsum('ptk,pkd->ptd', paired, dec_weight, preferred_element_type=jnp...]
    reduce_sum x1 -> x0, other arithmetic: 11.3 us -> none  [active_mask(): return jnp.sum((chosen[..., None] == columns).astype(jnp.float32), axis=2)]
    unnamed x18 -> x6, local copies, waits for them, and re-layouts: 2.76 us -> 7.64 us
    convert_element_type x3 -> x0, other arithmetic: 3.55 us -> none  [the longest x1 2.07 us: shards(): latents = (picked * jax.nn.softplus(preact)).astype(jnp.bfloat16)]
  transfers between devices with their start and end apart: 4 -> 0, of which waited for: 4 -> 0; matrix products, arithmetic and copies ran while one was open for 10% -> 0% of each run, Pallas kernels for 0% -> 0%
where the time goes in v1:
time: 57.5 us; the launch traced here: 57.3 us
  Pallas kernels  49 us (85%)
  local copies, waits for them, and re-layouts  7.64 us (13%)
  between operations  0.65 us (1%)
    pallas_call x1, Pallas kernels, shards(): pl.pallas_call(functools.partial(kernel, dims), out_shape=(jax.ShapeDtype...  49 us
    unnamed x6, local copies, waits for them, and re-layouts  7.64 us

profile of v1, /device:TPU:1, one launch (start us, length us, event | category | flops | bytes accessed | tf_op | source)
XLA Modules:
  0.0 57.3 jit_solution(388990371532831184)
XLA Ops:
  0.6 1.4 %copy.10.table = s32[9,2]{1,0:T(8,128)} copy(s32[9,2]{0,1:T(2,128)} %param.11) | data formatting | bytes 144 | tf_op args[4]
  2.0 1.9 %copy.9.topk_hbm = s32[2,512,64]{2,1,0:T(8,128)} copy(s32[2,512,64]{1,2,0:T(8,128)} %param.10) | data formatting | bytes 524288 | tf_op args[3]
  3.9 49.0 %transcoder_step.1 = (bf16[9,128,1024]{2,1,0:T(8,128)(2,1)}, f32[2,1024,128]{2,1,0:T(8,128)}) custom-call(bf16[2,512,1024]{2,1,0:T(8,128)(2,1)} %source_hbm.1, bf16[2,1024,128]{2,1,0:T(8,128)(2,1)} %encw_hbm.1, f32[2,128]{1,0:T(2,128)} %offset_hbm.1, s32[2,512,64]{2,1,0:T(8,128)} %copy.9.topk_hbm, s32[9,2]{1,0:T(8,128)} %copy.10.table, ...), custom_call_target="tpu_custom_call" | custom-call | flops 5368709120 | bytes 13107200 | tf_op jit(solution)/shard_map/transcoder_step/pallas_call | solution.py:316
  52.9 0.0 copy-start
  52.9 3.4 %copy.13 = bf16[9,128,1024]{2,1,0:T(8,128)(2,1)} copy(bf16[9,128,1024]{2,1,0:T(8,128)(2,1)} %get-tuple-element.4) | data formatting | bytes 4718592
  56.3 0.0 copy-done
  56.3 1.0 %copy.14 = f32[2,1024,128]{2,1,0:T(8,128)} copy(f32[2,1024,128]{2,1,0:T(8,128)S(1)} %copy-done) | data formatting | bytes 2097152
Async XLA Ops:
  52.9 3.4 %copy-start = (f32[2,1024,128]{2,1,0:T(8,128)S(1)}, f32[2,1024,128]{2,1,0:T(8,128)}, u32[]{:S(2)}) copy-start(f32[2,1024,128]{2,1,0:T(8,128)} %get-tuple-element.5) | copy-start | bytes 3145732

commit v2 on v1

--- a/solution.py
+++ b/solution.py
@@ -73,7 +73,7 @@
     for l in range(own):
         load(("s", l), source_hbm.at[l], source.at[l], 2 * l)
         load(("e", l), encw_hbm.at[l], encw.at[l], 2 * l + 1)
-    load("topk", topk_hbm.at[:, my_rows], topk, 2 * own)
+    load("topk", topk_hbm, topk, 2 * own)
     load("offset", offset_hbm, offset, 2 * own + 1)
     load("decw", decw_hbm, decw.at[pl.ds(0, pairs)], 2 * own + 2)
     load("target", target_hbm, target, 2 * own + 3)
@@ -90,8 +90,8 @@
         loads[("s", l)].wait()
         loads[("e", l)].wait()
         part[l] = jnp.dot(source[l], encw[l], preferred_element_type=F32)
-        if l == 0:
-            pl.semaphore_wait(barrier, n_t + n_z - 1)
+    pl.semaphore_wait(barrier, n_t + n_z - 1)
+    for l in range(own):
         core_copies.append(remote(
             part.at[l, half_rows(other)], part_core.at[l], pc_s.at[l], pc_r.at[l], width=other))
     x_copies = []
@@ -105,32 +105,31 @@
 
     loads["topk"].wait()
     loads["offset"].wait()
-    block = 32
-
-    for l in range(own):
-        @pl.loop(0, chunk // block)
-        def _(i, l=l):
-            rows = pl.ds(pl.multiple_of(i * block, block), block)
-            ids = topk[l, rows, :]
-            columns = lax.broadcasted_iota(jnp.int32, (block, latents), 1)
-            hit = jnp.zeros((block, latents), F32)
-            for k in range(topk.shape[2]):
-                hit = jnp.where(ids[:, k : k + 1] == columns, 1.0, hit)
-            picked[l, rows, :] = hit
-
-    high_target = table[0, 1]
+    span = picked.shape[1]
+    first_row = w * half + t * chunk
+    start = first_row // span * span
+    mask_rows = pl.ds(pl.multiple_of(first_row - start, chunk), chunk)
+    for l in range(own):
+        ids = topk[l, :, pl.ds(pl.multiple_of(start, span), span)]
+        names = lax.broadcasted_iota(jnp.int32, (latents, span), 0)
+        hit = jnp.zeros((latents, span), F32)
+        for k in range(topk.shape[1]):
+            hit = jnp.where(ids[k : k + 1, :] == names, 1.0, hit)
+        picked[l] = hit.T
+
+    high_target = table[1, 0]
     for p in range(1, pairs):
-        high_target = jnp.maximum(high_target, table[p, 1])
+        high_target = jnp.maximum(high_target, table[1, p])
     for p in range(pairs):
-        slot_of[p] = (table[p, 1] == high_target).astype(jnp.int32)
+        slot_of[p] = (table[1, p] == high_target).astype(jnp.int32)
 
     @pl.loop(0, layers)
     def _(l):
         high = jnp.int32(pairs)
         low = jnp.int32(pairs)
         for p in range(pairs):
-            same = table[p, 0] == l
-            up = table[p, 1] == high_target
+            same = table[0, p] == l
+            up = table[1, p] == high_target
             high = jnp.where(jnp.logical_and(same, up), p, high)
             low = jnp.where(jnp.logical_and(same, jnp.logical_not(up)), p, low)
         high_pair[l] = high
@@ -143,7 +142,7 @@
             pre = pre + part_x[l, d - 1]
         preact[l] = pre
         soft = jnp.maximum(pre, 0.0) + jnp.log1p(jnp.exp(-jnp.abs(pre)))
-        lat[z * own + l, my_rows, :] = (picked[l] * soft).astype(BF16)
+        lat[z * own + l, my_rows, :] = (picked[l, mask_rows, :] * soft).astype(BF16)
 
     z_copies = [None]
     for d in range(1, n_z):
@@ -151,12 +150,16 @@
         z_copies.append(remote(here, here, lz_s.at[d - 1], lz_r.at[d - 1], layer=z_peer(d)))
     x_copies = []
     for j in range(n_z):
+        if j == 1:
+            source_t[0] = source[0].T
         if j:
             z_copies[j].wait_recv()
         for d in range(1, n_t):
             here = lat.at[z_layers(z_from(j)), my_rows]
             x_copies.append(remote(
                 here, here, lx_s.at[j, d - 1], lx_r.at[j, d - 1], token=x_peer(d)))
+    for l in range(1, own):
+        source_t[l] = source[l].T
     loads["decw"].wait()
     decw[pairs] = jnp.zeros((latents, width), BF16)
     core_copies = []
@@ -165,28 +168,33 @@
             x_copies[j * (n_t - 1) + d - 1].wait_recv()
         here = lat.at[z_layers(z_from(j)), my_half]
         core_copies.append(remote(here, here, lc_s.at[j], lc_r.at[j], width=other))
-    for l in range(own):
-        source_t[l] = source[l].T
     loads["target"].wait()
+
+    tile = 256
+    lows = layers // 2
+
+    def decode(rows):
+        @pl.loop(0, width // tile)
+        def _(n):
+            cols = pl.ds(pl.multiple_of(n * tile, tile), tile)
+            for slot, count, pair_of in ((1, layers, high_pair), (0, lows, low_pair)):
+                acts = jnp.concatenate([lat[l, rows, :] for l in range(count)], axis=1)
+                weight = jnp.concatenate([decw[pair_of[l], :, cols] for l in range(count)], axis=0)
+                rebuilt = jnp.dot(acts, weight, preferred_element_type=F32)
+                goal = target[slot, rows, cols].astype(F32)
+                err[slot, rows, cols] = ((rebuilt - goal) * grad_scale).astype(BF16)
+
+    decode(my_half)
     for j in range(n_z):
         core_copies[j].wait_recv()
-
-    tile = 256
-    lows = layers // 2
-
-    @pl.loop(0, width // tile)
-    def _(n):
-        cols = pl.ds(pl.multiple_of(n * tile, tile), tile)
-        for slot, count, pair_of in ((1, layers, high_pair), (0, lows, low_pair)):
-            acts = jnp.concatenate([lat[l] for l in range(count)], axis=1)
-            weight = jnp.concatenate([decw[pair_of[l], :, cols] for l in range(count)], axis=0)
-            rebuilt = jnp.dot(acts, weight, preferred_element_type=F32)
-            goal = target[slot, :, cols].astype(F32)
-            err[slot, :, cols] = ((rebuilt - goal) * grad_scale).astype(BF16)
+    decode(half_rows(other))
 
     order = list(range(1, n_z)) + [0]
     core_copies = {}
-    for j in order:
+    x_copies = {}
+    z_copies = {}
+
+    def spread_to(j):
         zz = z_peer(j)
         weight = jnp.concatenate(
             [
@@ -202,8 +210,8 @@
             back[j, i] = spread[:, i * latents : (i + 1) * latents]
         core_copies[j] = remote(
             back.at[j, :, half_rows(other)], back_core.at[j], bc_s.at[j], bc_r.at[j], width=other)
-    x_copies = {}
-    for j in order:
+
+    def send_x(j):
         core_copies[j].wait_recv()
         total = back[j, :, my_half, :] + back_core[j]
         back[j, :, my_half, :] = total
@@ -214,18 +222,7 @@
                 back_xs.at[j, :, rows], back_x.at[j, d - 1],
                 bx_s.at[j, d - 1], bx_r.at[j, d - 1], token=x_peer(d))
 
-    def dec_gradient(first, last):
-        @pl.loop(first, last)
-        def _(p):
-            acts = lat[table[p, 0]].T
-            grad = jnp.dot(acts, err[slot_of[p]], preferred_element_type=F32)
-            dec_out[p] = grad.astype(BF16)
-            pltpu.make_async_copy(dec_out.at[p], decgrad_hbm.at[p], out_sem.at[p]).start()
-
-    middle = pairs // 2
-    dec_gradient(0, middle)
-    z_copies = {}
-    for j in order:
+    def send_z(j):
         total = back[j, :, my_rows, :]
         for d in range(1, n_t):
             x_copies[j, d].wait_recv()
@@ -234,14 +231,29 @@
             back_zs[j - 1] = total.astype(BF16)
             z_copies[j] = remote(
                 back_zs.at[j - 1], back_z.at[j - 1], bz_s.at[j - 1], bz_r.at[j - 1], layer=z_peer(j))
-        else:
-            mine = total
-    dec_gradient(middle, pairs)
+        return total
+
+    def dec_gradient(first, last):
+        @pl.loop(first, last)
+        def _(p):
+            acts = lat[table[0, p]].T
+            grad = jnp.dot(acts, err[slot_of[p]], preferred_element_type=F32)
+            dec_out[p] = grad.astype(BF16)
+            pltpu.make_async_copy(dec_out.at[p], decgrad_hbm.at[p], out_sem.at[p]).start()
+
+    spread_to(order[0])
+    for step in range(1, n_z):
+        spread_to(order[step])
+        send_x(order[step - 1])
+    send_x(order[-1])
+    for step in range(n_z):
+        dec_gradient(step * pairs // n_z, (step + 1) * pairs // n_z)
+        mine = send_z(order[step])
     for j in range(1, n_z):
         z_copies[j].wait_recv()
         mine = mine + back_z[j - 1].astype(F32)
     for l in range(own):
-        pre_grad[l, my_rows, :] = (mine[l] * picked[l] * jax.nn.sigmoid(preact[l])).astype(BF16)
+        pre_grad[l, my_rows, :] = (mine[l] * picked[l, mask_rows, :] * jax.nn.sigmoid(preact[l])).astype(BF16)
 
     here = pre_grad.at[:, my_rows]
     x_copies = [
@@ -250,9 +262,15 @@
     for copy in x_copies:
         copy.wait_recv()
     here = pre_grad.at[:, my_half]
-    remote(here, here, gc_s.at[0], gc_r.at[0], width=other).wait_recv()
-    for l in range(own):
-        enc_out[l] = jnp.dot(source_t[l], pre_grad[l], preferred_element_type=F32)
+    core_copy = remote(here, here, gc_s.at[0], gc_r.at[0], width=other)
+    for l in range(own):
+        enc_out[l] = jnp.dot(
+            source_t[l, :, my_half], pre_grad[l, my_half, :], preferred_element_type=F32)
+    core_copy.wait_recv()
+    rest = half_rows(other)
+    for l in range(own):
+        enc_out[l] = enc_out[l] + jnp.dot(
+            source_t[l, :, rest], pre_grad[l, rest, :], preferred_element_type=F32)
         pltpu.make_async_copy(enc_out.at[l], encgrad_hbm.at[l], out_sem.at[pairs + l]).start()
     for copy in sends:
         copy.wait_send()
@@ -282,14 +300,14 @@
         pltpu.VMEM((own, width, tokens), BF16),
         pltpu.VMEM((own, width, latents), BF16),
         pltpu.VMEM((own, latents), F32),
-        pltpu.VMEM((own, chunk, topk), jnp.int32),
+        pltpu.VMEM((own, topk, tokens), jnp.int32),
         pltpu.VMEM((pairs + 1, latents, width), BF16),
         pltpu.VMEM((2, tokens, width), BF16),
         pltpu.VMEM((own, tokens, latents), F32),
         pltpu.VMEM((own, half, latents), F32),
         pltpu.VMEM((own, peers, chunk, latents), F32),
         pltpu.VMEM((own, chunk, latents), F32),
-        pltpu.VMEM((own, chunk, latents), F32),
+        pltpu.VMEM((own, max(chunk, 128), latents), F32),
         pltpu.VMEM((layers, tokens, latents), BF16),
         pltpu.VMEM((2, tokens, width), BF16),
         pltpu.VMEM((n_z, own, tokens, latents), F32),
@@ -313,7 +331,7 @@
     ):
         scratch += [dma(shape), dma(shape)]
     hbm = pl.BlockSpec(memory_space=pl.ANY)
-    return pl.pallas_call(
+    grads = pl.pallas_call(
         functools.partial(kernel, dims),
         out_shape=(
             jax.ShapeDtypeStruct((pairs, latents, width), BF16),
@@ -331,7 +349,37 @@
             transcendentals=0,
         ),
         name="transcoder_step",
-    )(source_acts, enc_weight, enc_offset, topk_latents, pair_table, dec_weight, target_acts)
+    )(
+        source_acts, enc_weight, enc_offset, jnp.swapaxes(topk_latents, 1, 2), pair_table.T,
+        dec_weight, target_acts,
+    )
+    return write_out(*grads)
+
+
+def write_kernel(dec_in, enc_in, dec_out, enc_out, sem):
+    copies = [pltpu.make_async_copy(dec_in.at[p], dec_out.at[p], sem.at[p]) for p in range(dec_in.shape[0])]
+    copies += [
+        pltpu.make_async_copy(enc_in.at[l], enc_out.at[l], sem.at[len(copies) + l])
+        for l in range(enc_in.shape[0])
+    ]
+    for copy in copies:
+        copy.start()
+    for copy in copies:
+        copy.wait()
+
+
+def write_out(dec, enc):
+    hbm = pl.BlockSpec(memory_space=pl.ANY)
+    return pl.pallas_call(
+        write_kernel,
+        out_shape=(
+            jax.ShapeDtypeStruct(dec.shape, dec.dtype), jax.ShapeDtypeStruct(enc.shape, enc.dtype)
+        ),
+        in_specs=[hbm, hbm],
+        out_specs=(hbm, hbm),
+        scratch_shapes=[pltpu.SemaphoreType.DMA((dec.shape[0] + enc.shape[0],))],
+        name="write_out",
+    )(dec, enc)
 
 
 def solution(mesh):

time: 57.5 us -> 153 us (2.66)
  Pallas kernels: 49 us -> 152 us
  local copies, waits for them, and re-layouts: 7.64 us -> 0 us
    pallas_call x0 -> x1, Pallas kernels: none -> 104 us  [write_out(): pl.pallas_call(write_kernel, out_shape=(jax.ShapeDtypeStruct(dec.shape, d...]
    unnamed x6 -> x0, local copies, waits for them, and re-layouts: 7.64 us -> none
where the time goes in v2:
time: 153 us
  Pallas kernels  152 us (99%)
    pallas_call x1, Pallas kernels, write_out(): pl.pallas_call(write_kernel, out_shape=(jax.ShapeDtypeStruct(dec.shape, d...  104 us
    pallas_call x1, Pallas kernels, shards(): pl.pallas_call(functools.partial(kernel, dims), out_shape=(jax.ShapeDtype...  47.9 us

profile of v2, /device:TPU:1, one launch (start us, length us, event | category | flops | bytes accessed | tf_op | source)
XLA Modules:
  0.0 153.0 jit_solution(2144889111698465567)
XLA Ops:
  0.6 47.9 %transcoder_step.1 = (bf16[9,128,1024]{2,1,0:T(8,128)(2,1)}, f32[2,1024,128]{2,1,0:T(8,128)}) custom-call(bf16[2,512,1024]{2,1,0:T(8,128)(2,1)} %source_hbm.1, bf16[2,1024,128]{2,1,0:T(8,128)(2,1)} %encw_hbm.1, f32[2,128]{1,0:T(2,128)} %offset_hbm.1, s32[2,64,512]{2,1,0:T(8,128)} %bitcast.2, s32[2,9]{1,0:T(2,128)} %bitcast.3, ...), custom_call_target="tpu_custom_call" | custom-call | flops 5368709120 | bytes 13107200 | tf_op jit(solution)/shard_map/transcoder_step/pallas_call | solution.py:334
  48.5 104.4 %write_out.1 = (bf16[9,128,1024]{2,1,0:T(8,128)(2,1)}, f32[2,1024,128]{2,1,0:T(8,128)}) custom-call(bf16[9,128,1024]{2,1,0:T(8,128)(2,1)} %get-tuple-element.4.dec_in, f32[2,1024,128]{2,1,0:T(8,128)} %get-tuple-element.5.enc_in), custom_call_target="tpu_custom_call" | custom-call | tf_op jit(solution)/shard_map/write_out/pallas_call | solution.py:373

commit v3 on v2

--- a/solution.py
+++ b/solution.py
@@ -356,16 +356,19 @@
     return write_out(*grads)
 
 
-def write_kernel(dec_in, enc_in, dec_out, enc_out, sem):
-    copies = [pltpu.make_async_copy(dec_in.at[p], dec_out.at[p], sem.at[p]) for p in range(dec_in.shape[0])]
-    copies += [
-        pltpu.make_async_copy(enc_in.at[l], enc_out.at[l], sem.at[len(copies) + l])
-        for l in range(enc_in.shape[0])
-    ]
-    for copy in copies:
-        copy.start()
-    for copy in copies:
-        copy.wait()
+def write_kernel(dec_in, enc_in, dec_out, enc_out, dec, enc, in_sem, out_sem):
+    pairs, own = dec.shape[0], enc.shape[0]
+    moves = [(dec_in.at[p], dec.at[p], dec_out.at[p]) for p in range(pairs)]
+    moves += [(enc_in.at[l], enc.at[l], enc_out.at[l]) for l in range(own)]
+    loads = [pltpu.make_async_copy(a, b, in_sem.at[i]) for i, (a, b, _) in enumerate(moves)]
+    stores = [pltpu.make_async_copy(b, c, out_sem.at[i]) for i, (_, b, c) in enumerate(moves)]
+    for load in loads:
+        load.start()
+    for load, store in zip(loads, stores):
+        load.wait()
+        store.start()
+    for store in stores:
+        store.wait()
 
 
 def write_out(dec, enc):
@@ -377,7 +380,13 @@
         ),
         in_specs=[hbm, hbm],
         out_specs=(hbm, hbm),
-        scratch_shapes=[pltpu.SemaphoreType.DMA((dec.shape[0] + enc.shape[0],))],
+        scratch_shapes=[
+            pltpu.VMEM(dec.shape, dec.dtype),
+            pltpu.VMEM(enc.shape, enc.dtype),
+            pltpu.SemaphoreType.DMA((dec.shape[0] + enc.shape[0],)),
+            pltpu.SemaphoreType.DMA((dec.shape[0] + enc.shape[0],)),
+        ],
+        compiler_params=pltpu.CompilerParams(vmem_limit_bytes=56 * 1024 * 1024),
         name="write_out",
     )(dec, enc)
 

time: 153 us -> 51.7 us (0.34)
  Pallas kernels: 152 us -> 50.9 us
    pallas_call x1, Pallas kernels: 104 us -> 3.04 us  [write_out(): pl.pallas_call(write_kernel, out_shape=(jax.ShapeDtypeStruct(dec.shape, d...]
where the time goes in v3:
time: 51.7 us; the launch traced here: 51.6 us
  Pallas kernels  50.9 us (98%)
  between operations  0.64 us (1%)
    pallas_call x1, Pallas kernels, shards(): pl.pallas_call(functools.partial(kernel, dims), out_shape=(jax.ShapeDtype...  47.9 us
    pallas_call x1, Pallas kernels, write_out(): pl.pallas_call(write_kernel, out_shape=(jax.ShapeDtypeStruct(dec.shape, d...  3.04 us

profile of v3, /device:TPU:1, one launch (start us, length us, event | category | flops | bytes accessed | tf_op | source)
XLA Modules:
  0.0 51.6 jit_solution(11798092175497100651)
XLA Ops:
  0.6 47.9 %transcoder_step.1 = (bf16[9,128,1024]{2,1,0:T(8,128)(2,1)}, f32[2,1024,128]{2,1,0:T(8,128)}) custom-call(bf16[2,512,1024]{2,1,0:T(8,128)(2,1)} %source_hbm.1, bf16[2,1024,128]{2,1,0:T(8,128)(2,1)} %encw_hbm.1, f32[2,128]{1,0:T(2,128)} %offset_hbm.1, s32[2,64,512]{2,1,0:T(8,128)} %bitcast.2, s32[2,9]{1,0:T(2,128)} %bitcast.3, ...), custom_call_target="tpu_custom_call" | custom-call | flops 5368709120 | bytes 13107200 | tf_op jit(solution)/shard_map/transcoder_step/pallas_call | solution.py:334
  48.5 3.0 %write_out.1 = (bf16[9,128,1024]{2,1,0:T(8,128)(2,1)}, f32[2,1024,128]{2,1,0:T(8,128)}) custom-call(bf16[9,128,1024]{2,1,0:T(8,128)(2,1)} %get-tuple-element.4.dec_in, f32[2,1024,128]{2,1,0:T(8,128)} %get-tuple-element.5.enc_in), custom_call_target="tpu_custom_call" | custom-call | tf_op jit(solution)/shard_map/write_out/pallas_call | solution.py:376

commit v4 on v3

--- a/solution.py
+++ b/solution.py
@@ -94,12 +94,12 @@
     for l in range(own):
         core_copies.append(remote(
             part.at[l, half_rows(other)], part_core.at[l], pc_s.at[l], pc_r.at[l], width=other))
-    x_copies = []
+    first_copies = []
     for l in range(own):
         core_copies[l].wait_recv()
         part[l, my_half, :] = part[l, my_half, :] + part_core[l]
         for d in range(1, n_t):
-            x_copies.append(remote(
+            first_copies.append(remote(
                 part.at[l, chunk_rows(x_peer(d), w)], part_x.at[l, d - 1],
                 px_s.at[l, d - 1], px_r.at[l, d - 1], token=x_peer(d)))
 
@@ -135,37 +135,43 @@
         high_pair[l] = high
         low_pair[l] = low
 
+    z_copies = {}
+    x_copies = {}
+
+    def pass_x(j, l):
+        for d in range(1, n_t):
+            here = lat.at[z_from(j) * own + l, my_rows]
+            x_copies[j, l, d] = remote(
+                here, here, lx_s.at[j, l, d - 1], lx_r.at[j, l, d - 1], token=x_peer(d))
+
     for l in range(own):
         pre = part[l, my_rows, :] + offset[pl.ds(l, 1), :]
         for d in range(1, n_t):
-            x_copies[l * (n_t - 1) + d - 1].wait_recv()
+            first_copies[l * (n_t - 1) + d - 1].wait_recv()
             pre = pre + part_x[l, d - 1]
         preact[l] = pre
         soft = jnp.maximum(pre, 0.0) + jnp.log1p(jnp.exp(-jnp.abs(pre)))
         lat[z * own + l, my_rows, :] = (picked[l, mask_rows, :] * soft).astype(BF16)
 
-    z_copies = [None]
-    for d in range(1, n_z):
-        here = lat.at[z_layers(z), my_rows]
-        z_copies.append(remote(here, here, lz_s.at[d - 1], lz_r.at[d - 1], layer=z_peer(d)))
-    x_copies = []
-    for j in range(n_z):
-        if j == 1:
-            source_t[0] = source[0].T
-        if j:
-            z_copies[j].wait_recv()
-        for d in range(1, n_t):
-            here = lat.at[z_layers(z_from(j)), my_rows]
-            x_copies.append(remote(
-                here, here, lx_s.at[j, d - 1], lx_r.at[j, d - 1], token=x_peer(d)))
+        for d in range(1, n_z):
+            here = lat.at[z * own + l, my_rows]
+            z_copies[d, l] = remote(
+                here, here, lz_s.at[d - 1, l], lz_r.at[d - 1, l], layer=z_peer(d))
+        pass_x(0, l)
+    source_t[0] = source[0].T
+    for j in range(1, n_z):
+        for l in range(own):
+            z_copies[j, l].wait_recv()
+            pass_x(j, l)
     for l in range(1, own):
         source_t[l] = source[l].T
     loads["decw"].wait()
     decw[pairs] = jnp.zeros((latents, width), BF16)
     core_copies = []
     for j in range(n_z):
-        for d in range(1, n_t):
-            x_copies[j * (n_t - 1) + d - 1].wait_recv()
+        for l in range(own):
+            for d in range(1, n_t):
+                x_copies[j, l, d].wait_recv()
         here = lat.at[z_layers(z_from(j)), my_half]
         core_copies.append(remote(here, here, lc_s.at[j], lc_r.at[j], width=other))
     loads["target"].wait()
@@ -196,18 +202,21 @@
 
     def spread_to(j):
         zz = z_peer(j)
-        weight = jnp.concatenate(
-            [
-                jnp.concatenate([decw[high_pair[zz * own + i]], decw[low_pair[zz * own + i]]], axis=1)
-                for i in range(own)
-            ],
-            axis=0,
-        )
-        both = jnp.concatenate([err[1], err[0]], axis=1)
-        spread = lax.dot_general(
-            both, weight, (((1,), (1,)), ((), ())), preferred_element_type=F32)
+        def times(slot, pair_of):
+            weight = jnp.concatenate([decw[pair_of[zz * own + i]] for i in range(own)], axis=0)
+            return lax.dot_general(
+                err[slot], weight, (((1,), (1,)), ((), ())), preferred_element_type=F32)
+
+        spread = times(1, high_pair)
         for i in range(own):
             back[j, i] = spread[:, i * latents : (i + 1) * latents]
+
+        @pl.when(zz * own < lows)
+        def _():
+            spread = times(0, low_pair)
+            for i in range(own):
+                back[j, i] = back[j, i] + spread[:, i * latents : (i + 1) * latents]
+
         core_copies[j] = remote(
             back.at[j, :, half_rows(other)], back_core.at[j], bc_s.at[j], bc_r.at[j], width=other)
 
@@ -247,8 +256,8 @@
         send_x(order[step - 1])
     send_x(order[-1])
     for step in range(n_z):
+        mine = send_z(order[step])
         dec_gradient(step * pairs // n_z, (step + 1) * pairs // n_z)
-        mine = send_z(order[step])
     for j in range(1, n_z):
         z_copies[j].wait_recv()
         mine = mine + back_z[j - 1].astype(F32)
@@ -326,7 +335,7 @@
         dma((pairs + own,)),
     ]
     for shape in (
-        (own,), (own, peers), (others,), (n_z, peers), (n_z,),
+        (own,), (own, peers), (others, own), (n_z, own, peers), (n_z,),
         (n_z,), (n_z, peers), (others,), (peers,), (1,),
     ):
         scratch += [dma(shape), dma(shape)]

time: 51.7 us -> 48.1 us (0.930)
  Pallas kernels: 50.9 us -> 47.3 us
    pallas_call x1, Pallas kernels: 47.9 us -> 44.3 us  [shards(): pl.pallas_call(functools.partial(kernel, dims), out_shape=(jax.ShapeDtype...]
where the time goes in v4:
time: 48.1 us; the launch traced here: 47.9 us
  Pallas kernels  47.3 us (98%)
  between operations  0.64 us (1%)
    pallas_call x1, Pallas kernels, shards(): pl.pallas_call(functools.partial(kernel, dims), out_shape=(jax.ShapeDtype...  44.3 us
    pallas_call x1, Pallas kernels, write_out(): pl.pallas_call(write_kernel, out_shape=(jax.ShapeDtypeStruct(dec.shape, d...  3.04 us

profile of v4, /device:TPU:1, one launch (start us, length us, event | category | flops | bytes accessed | tf_op | source)
XLA Modules:
  0.0 47.9 jit_solution(14751013777220775554)
XLA Ops:
  0.6 44.3 %transcoder_step.1 = (bf16[9,128,1024]{2,1,0:T(8,128)(2,1)}, f32[2,1024,128]{2,1,0:T(8,128)}) custom-call(bf16[2,512,1024]{2,1,0:T(8,128)(2,1)} %source_hbm.1, bf16[2,1024,128]{2,1,0:T(8,128)(2,1)} %encw_hbm.1, f32[2,128]{1,0:T(2,128)} %offset_hbm.1, s32[2,64,512]{2,1,0:T(8,128)} %bitcast.2, s32[2,9]{1,0:T(2,128)} %bitcast.3, ...), custom_call_target="tpu_custom_call" | custom-call | flops 5368709120 | bytes 13107200 | tf_op jit(solution)/shard_map/transcoder_step/pallas_call | solution.py:343
  44.9 3.0 %write_out.1 = (bf16[9,128,1024]{2,1,0:T(8,128)(2,1)}, f32[2,1024,128]{2,1,0:T(8,128)}) custom-call(bf16[9,128,1024]{2,1,0:T(8,128)(2,1)} %get-tuple-element.4.dec_in, f32[2,1024,128]{2,1,0:T(8,128)} %get-tuple-element.5.enc_in), custom_call_target="tpu_custom_call" | custom-call | tf_op jit(solution)/shard_map/write_out/pallas_call | solution.py:385

commit v5 on v4

--- a/solution.py
+++ b/solution.py
@@ -202,45 +202,54 @@
 
     def spread_to(j):
         zz = z_peer(j)
-        def times(slot, pair_of):
+        def times(slot, pair_of, rows):
             weight = jnp.concatenate([decw[pair_of[zz * own + i]] for i in range(own)], axis=0)
             return lax.dot_general(
-                err[slot], weight, (((1,), (1,)), ((), ())), preferred_element_type=F32)
-
-        spread = times(1, high_pair)
-        for i in range(own):
-            back[j, i] = spread[:, i * latents : (i + 1) * latents]
-
-        @pl.when(zz * own < lows)
-        def _():
-            spread = times(0, low_pair)
+                err[slot, rows, :], weight, (((1,), (1,)), ((), ())), preferred_element_type=F32)
+
+        def half_spread(rows):
+            spread = times(1, high_pair, rows)
             for i in range(own):
-                back[j, i] = back[j, i] + spread[:, i * latents : (i + 1) * latents]
-
+                back[j, i, rows, :] = spread[:, i * latents : (i + 1) * latents]
+
+            @pl.when(zz * own < lows)
+            def _():
+                spread = times(0, low_pair, rows)
+                for i in range(own):
+                    back[j, i, rows, :] = (
+                        back[j, i, rows, :] + spread[:, i * latents : (i + 1) * latents])
+
+        half_spread(half_rows(other))
         core_copies[j] = remote(
             back.at[j, :, half_rows(other)], back_core.at[j], bc_s.at[j], bc_r.at[j], width=other)
+        half_spread(my_half)
 
     def send_x(j):
         core_copies[j].wait_recv()
-        total = back[j, :, my_half, :] + back_core[j]
-        back[j, :, my_half, :] = total
-        back_xs[j] = total.astype(BF16)
-        for d in range(1, n_t):
-            rows = pl.ds(pl.multiple_of(x_peer(d) * chunk, chunk), chunk)
-            x_copies[j, d] = remote(
-                back_xs.at[j, :, rows], back_x.at[j, d - 1],
-                bx_s.at[j, d - 1], bx_r.at[j, d - 1], token=x_peer(d))
+        for i in range(own):
+            total = back[j, i, my_half, :] + back_core[j, i]
+            back[j, i, my_half, :] = total
+            back_xs[j, i] = total.astype(BF16)
+            for d in range(1, n_t):
+                rows = pl.ds(pl.multiple_of(x_peer(d) * chunk, chunk), chunk)
+                x_copies[j, i, d] = remote(
+                    back_xs.at[j, i, rows], back_x.at[j, d - 1, i],
+                    bx_s.at[j, d - 1, i], bx_r.at[j, d - 1, i], token=x_peer(d))
 
     def send_z(j):
-        total = back[j, :, my_rows, :]
-        for d in range(1, n_t):
-            x_copies[j, d].wait_recv()
-            total = total + back_x[j, d - 1].astype(F32)
-        if j:
-            back_zs[j - 1] = total.astype(BF16)
-            z_copies[j] = remote(
-                back_zs.at[j - 1], back_z.at[j - 1], bz_s.at[j - 1], bz_r.at[j - 1], layer=z_peer(j))
-        return total
+        totals = []
+        for i in range(own):
+            total = back[j, i, my_rows, :]
+            for d in range(1, n_t):
+                x_copies[j, i, d].wait_recv()
+                total = total + back_x[j, d - 1, i].astype(F32)
+            totals.append(total)
+            if j:
+                back_zs[j - 1, i] = total.astype(BF16)
+                z_copies[j, i] = remote(
+                    back_zs.at[j - 1, i], back_z.at[j - 1, i],
+                    bz_s.at[j - 1, i], bz_r.at[j - 1, i], layer=z_peer(j))
+        return totals
 
     def dec_gradient(first, last):
         @pl.loop(first, last)
@@ -258,26 +267,30 @@
     for step in range(n_z):
         mine = send_z(order[step])
         dec_gradient(step * pairs // n_z, (step + 1) * pairs // n_z)
-    for j in range(1, n_z):
-        z_copies[j].wait_recv()
-        mine = mine + back_z[j - 1].astype(F32)
-    for l in range(own):
-        pre_grad[l, my_rows, :] = (mine[l] * picked[l, mask_rows, :] * jax.nn.sigmoid(preact[l])).astype(BF16)
-
-    here = pre_grad.at[:, my_rows]
-    x_copies = [
-        remote(here, here, gx_s.at[d - 1], gx_r.at[d - 1], token=x_peer(d)) for d in range(1, n_t)
-    ]
-    for copy in x_copies:
-        copy.wait_recv()
-    here = pre_grad.at[:, my_half]
-    core_copy = remote(here, here, gc_s.at[0], gc_r.at[0], width=other)
+    g_copies = {}
+    for l in range(own):
+        grad = mine[l]
+        for j in range(1, n_z):
+            z_copies[j, l].wait_recv()
+            grad = grad + back_z[j - 1, l].astype(F32)
+        pre_grad[l, my_rows, :] = (
+            grad * picked[l, mask_rows, :] * jax.nn.sigmoid(preact[l])).astype(BF16)
+        here = pre_grad.at[l, my_rows]
+        for d in range(1, n_t):
+            g_copies[l, d] = remote(
+                here, here, gx_s.at[d - 1, l], gx_r.at[d - 1, l], token=x_peer(d))
+    core_copies = []
+    for l in range(own):
+        for d in range(1, n_t):
+            g_copies[l, d].wait_recv()
+        here = pre_grad.at[l, my_half]
+        core_copies.append(remote(here, here, gc_s.at[l], gc_r.at[l], width=other))
     for l in range(own):
         enc_out[l] = jnp.dot(
             source_t[l, :, my_half], pre_grad[l, my_half, :], preferred_element_type=F32)
-    core_copy.wait_recv()
     rest = half_rows(other)
     for l in range(own):
+        core_copies[l].wait_recv()
         enc_out[l] = enc_out[l] + jnp.dot(
             source_t[l, :, rest], pre_grad[l, rest, :], preferred_element_type=F32)
         pltpu.make_async_copy(enc_out.at[l], encgrad_hbm.at[l], out_sem.at[pairs + l]).start()
@@ -336,7 +349,7 @@
     ]
     for shape in (
         (own,), (own, peers), (others, own), (n_z, own, peers), (n_z,),
-        (n_z,), (n_z, peers), (others,), (peers,), (1,),
+        (n_z,), (n_z, peers, own), (others, own), (peers, own), (own,),
     ):
         scratch += [dma(shape), dma(shape)]
     hbm = pl.BlockSpec(memory_space=pl.ANY)

time: 48.1 us -> 47.7 us (level)
  Pallas kernels: 47.3 us -> 46.8 us
    pallas_call x1, Pallas kernels: 44.3 us -> 43.8 us  [shards(): pl.pallas_call(functools.partial(kernel, dims), out_shape=(jax.ShapeDtype...]
where the time goes in v5:
time: 47.7 us; the launch traced here: 47.5 us
  Pallas kernels  46.8 us (98%)
  between operations  0.64 us (1%)
    pallas_call x1, Pallas kernels, shards(): pl.pallas_call(functools.partial(kernel, dims), out_shape=(jax.ShapeDtype...  43.8 us
    pallas_call x1, Pallas kernels, write_out(): pl.pallas_call(write_kernel, out_shape=(jax.ShapeDtypeStruct(dec.shape, d...  3.04 us

profile of v5, /device:TPU:1, one launch (start us, length us, event | category | flops | bytes accessed | tf_op | source)
XLA Modules:
  0.0 47.5 jit_solution(17172085064226762137)
XLA Ops:
  0.6 43.8 %transcoder_step.1 = (bf16[9,128,1024]{2,1,0:T(8,128)(2,1)}, f32[2,1024,128]{2,1,0:T(8,128)}) custom-call(bf16[2,512,1024]{2,1,0:T(8,128)(2,1)} %source_hbm.1, bf16[2,1024,128]{2,1,0:T(8,128)(2,1)} %encw_hbm.1, f32[2,128]{1,0:T(2,128)} %offset_hbm.1, s32[2,64,512]{2,1,0:T(8,128)} %bitcast.2, s32[2,9]{1,0:T(2,128)} %bitcast.3, ...), custom_call_target="tpu_custom_call" | custom-call | flops 5368709120 | bytes 13107200 | tf_op jit(solution)/shard_map/transcoder_step/pallas_call | solution.py:356
  44.4 3.0 %write_out.1 = (bf16[9,128,1024]{2,1,0:T(8,128)(2,1)}, f32[2,1024,128]{2,1,0:T(8,128)}) custom-call(bf16[9,128,1024]{2,1,0:T(8,128)(2,1)} %get-tuple-element.4.dec_in, f32[2,1024,128]{2,1,0:T(8,128)} %get-tuple-element.5.enc_in), custom_call_target="tpu_custom_call" | custom-call | tf_op jit(solution)/shard_map/write_out/pallas_call | solution.py:398

commit v6 on v5

--- a/solution.py
+++ b/solution.py
@@ -158,15 +158,15 @@
             z_copies[d, l] = remote(
                 here, here, lz_s.at[d - 1, l], lz_r.at[d - 1, l], layer=z_peer(d))
         pass_x(0, l)
-    source_t[0] = source[0].T
+    for l in range(own):
+        source_t[l] = source[l].T
+    loads["decw"].wait()
+    decw[pairs] = jnp.zeros((latents, width), BF16)
+    loads["target"].wait()
     for j in range(1, n_z):
         for l in range(own):
             z_copies[j, l].wait_recv()
             pass_x(j, l)
-    for l in range(1, own):
-        source_t[l] = source[l].T
-    loads["decw"].wait()
-    decw[pairs] = jnp.zeros((latents, width), BF16)
     core_copies = []
     for j in range(n_z):
         for l in range(own):
@@ -174,8 +174,6 @@
                 x_copies[j, l, d].wait_recv()
         here = lat.at[z_layers(z_from(j)), my_half]
         core_copies.append(remote(here, here, lc_s.at[j], lc_r.at[j], width=other))
-    loads["target"].wait()
-
     tile = 256
     lows = layers // 2
 
@@ -195,7 +193,7 @@
         core_copies[j].wait_recv()
     decode(half_rows(other))
 
-    order = list(range(1, n_z)) + [0]
+    order = [n_z // 2] + [j for j in range(1, n_z) if j != n_z // 2] + [0]
     core_copies = {}
     x_copies = {}
     z_copies = {}

time: 47.7 us -> 46.9 us (0.983)
  Pallas kernels: 46.8 us -> 46 us
    pallas_call x1, Pallas kernels: 43.8 us -> 43 us  [shards(): pl.pallas_call(functools.partial(kernel, dims), out_shape=(jax.ShapeDtype...]
where the time goes in v6:
time: 46.9 us; the launch traced here: 46.7 us
  Pallas kernels  46 us (98%)
  between operations  0.64 us (1%)
    pallas_call x1, Pallas kernels, shards(): pl.pallas_call(functools.partial(kernel, dims), out_shape=(jax.ShapeDtype...  43 us
    pallas_call x1, Pallas kernels, write_out(): pl.pallas_call(write_kernel, out_shape=(jax.ShapeDtypeStruct(dec.shape, d...  3.04 us

profile of v6, /device:TPU:1, one launch (start us, length us, event | category | flops | bytes accessed | tf_op | source)
XLA Modules:
  0.0 46.7 jit_solution(15437922083199832121)
XLA Ops:
  0.6 43.0 %transcoder_step.1 = (bf16[9,128,1024]{2,1,0:T(8,128)(2,1)}, f32[2,1024,128]{2,1,0:T(8,128)}) custom-call(bf16[2,512,1024]{2,1,0:T(8,128)(2,1)} %source_hbm.1, bf16[2,1024,128]{2,1,0:T(8,128)(2,1)} %encw_hbm.1, f32[2,128]{1,0:T(2,128)} %offset_hbm.1, s32[2,64,512]{2,1,0:T(8,128)} %bitcast.2, s32[2,9]{1,0:T(2,128)} %bitcast.3, ...), custom_call_target="tpu_custom_call" | custom-call | flops 5368709120 | bytes 13107200 | tf_op jit(solution)/shard_map/transcoder_step/pallas_call | solution.py:354
  43.6 3.0 %write_out.1 = (bf16[9,128,1024]{2,1,0:T(8,128)(2,1)}, f32[2,1024,128]{2,1,0:T(8,128)}) custom-call(bf16[9,128,1024]{2,1,0:T(8,128)(2,1)} %get-tuple-element.4.dec_in, f32[2,1024,128]{2,1,0:T(8,128)} %get-tuple-element.5.enc_in), custom_call_target="tpu_custom_call" | custom-call | tf_op jit(solution)/shard_map/write_out/pallas_call | solution.py:396
